TPU v7x, 128 devices: a whole 4x4x4 slice. The times are simulated.
128 devices in a mesh: leaf: 16 (over y, z), row: 8 (over x, core).
Axes of the slice: x: 4, y: 4, z: 4, core: 2. Of those that a mesh axis runs over, the one named last changes fastest.
Arguments:
- panel0: float32 [24576, 512], P(('leaf', 'row')), may hold values from -3 to 30, as said below
- panel1: float32 [12288, 512], P(('leaf', 'row')), may hold values from -3 to 30
- panel2: float32 [6144, 512], P(('leaf', 'row')), may hold values from -3 to 30
- panel3: float32 [3072, 512], P(('leaf', 'row')), may hold values from -3 to 30
- maps1: int32 [16, 8], replicated, may hold values from 0 to 11, as said below
- maps2: int32 [8, 8], replicated, may hold values from 0 to 11, as said below
- maps3: int32 [4, 8], replicated, may hold values from 0 to 11, as said below
Outputs:
- update_top: float32 [2048, 1024], P(('leaf', 'row'))
Inputs may be any that keep to these rules, and one draw needn't show every extreme that they name: `panel0`: each front's first 512 rows form a symmetric matrix, and every assembled pivot block is positive definite. `maps1`: each row lists distinct parent block numbers. `maps2`: each row lists distinct parent block numbers. `maps3`: each row lists distinct parent block numbers.
All inputs are finite; a program needn't handle non-finite values.
Results may differ from a plain program's by a relative error of at most 0.0003.
Values sent between devices are 32-bit elements; how exact they have to be, the bound alone decides.
No kernel may reach another device: no remote copies, remote signals or barrier semaphores. Data moves between devices by JAX's collectives and lax.ppermute only.
A program may use at most 128 MiB of HBM per device.

v0:
```python
import jax
import jax.numpy as jnp
from jax import lax
from jax.sharding import PartitionSpec as P

BLOCK = 128
PIV = 512
UPD = 1024


exact_mode = lax.Precision.HIGHEST


def partner(block, axis, stride):
    count = lax.axis_size(axis)
    route = []
    for low in range(count):
        high = low | 1 << stride
        if high != low and high < count:
            route += [(low, high), (high, low)]
    return lax.ppermute(block, axis, route)


def extend_add(update, blocks):
    parent_blocks = (PIV + UPD) // BLOCK
    child_blocks = blocks.shape[0]
    onehot = (blocks[:, None] == jnp.arange(parent_blocks, dtype=jnp.int32)[None, :]).astype(
        jnp.float32
    )
    tile_grid = update.reshape(child_blocks, BLOCK, child_blocks, BLOCK)
    spread = jnp.einsum("ia,ixjy->axjy", onehot, tile_grid, precision=exact_mode)
    placed = jnp.einsum("axjy,jb->axby", spread, onehot, precision=exact_mode)
    return placed.reshape(parent_blocks * BLOCK, parent_blocks * BLOCK)


def exact_dot(left, right):
    return jnp.dot(left, right, precision=exact_mode, preferred_element_type=jnp.float32)


def inverse_factor(pivot_block):
    tile_count = PIV // BLOCK
    identity = jnp.eye(BLOCK, dtype=jnp.float32)
    remaining = pivot_block
    lower_tiles = {}
    diag_inverse = []
    for column_tile in range(tile_count):
        offset = column_tile * BLOCK
        diag_factor = jnp.linalg.cholesky(
            remaining[offset : offset + BLOCK, offset : offset + BLOCK]
        )
        tile_inverse = jax.scipy.linalg.solve_triangular(diag_factor, identity, lower=True)
        diag_inverse.append(tile_inverse)
        if column_tile + 1 < tile_count:
            below_rows = exact_dot(
                remaining[offset + BLOCK :, offset : offset + BLOCK], tile_inverse.T
            )
            for row_tile in range(column_tile + 1, tile_count):
                start_row = (row_tile - column_tile - 1) * BLOCK
                lower_tiles[row_tile, column_tile] = below_rows[start_row : start_row + BLOCK]
            trailing_part = remaining[offset + BLOCK :, offset + BLOCK :] - exact_dot(
                below_rows, below_rows.T
            )
            remaining = remaining.at[offset + BLOCK :, offset + BLOCK :].set(trailing_part)
    inverse_tiles = {}
    for column_tile in range(tile_count):
        inverse_tiles[column_tile, column_tile] = diag_inverse[column_tile]
        for row_tile in range(column_tile + 1, tile_count):
            accumulated = jnp.zeros((BLOCK, BLOCK), jnp.float32)
            for middle in range(column_tile, row_tile):
                accumulated = accumulated + exact_dot(
                    lower_tiles[row_tile, middle], inverse_tiles[middle, column_tile]
                )
            inverse_tiles[row_tile, column_tile] = -exact_dot(diag_inverse[row_tile], accumulated)
    zero_tile = jnp.zeros((BLOCK, BLOCK), jnp.float32)
    tile_rows = []
    for row_tile in range(tile_count):
        pieces = [
            inverse_tiles[row_tile, column_tile] if column_tile <= row_tile else zero_tile
            for column_tile in range(tile_count)
        ]
        tile_rows.append(jnp.concatenate(pieces, axis=1))
    return jnp.concatenate(tile_rows, axis=0)


def group_total(partial_value, level_index):
    assembled = lax.psum(partial_value, "row")
    for bit_number in range(level_index):
        assembled = assembled + partner(assembled, "leaf", bit_number)
    return assembled


def body(panel0, panel1, panel2, panel3, maps1, maps2, maps3):
    panels = (panel0, panel1, panel2, panel3)
    block_maps = (maps1, maps1, maps2, maps3)
    row_devices = lax.axis_size("row")
    leaf_index = lax.axis_index("leaf")
    row_index = lax.axis_index("row")
    schur = jnp.zeros((UPD, UPD), jnp.float32)
    for level_index in range(4):
        group_leaves = 2**level_index
        position = leaf_index % group_leaves * row_devices + row_index
        group_devices = group_leaves * row_devices
        panel_rows = panels[level_index]
        row_count = panel_rows.shape[0]
        if level_index == 0:
            partial_value = jnp.zeros((PIV + UPD, PIV), jnp.float32)
            trailing = jnp.zeros((UPD, UPD), jnp.float32)
        else:
            child_front = leaf_index // (group_leaves // 2)
            blocks = lax.dynamic_index_in_dim(
                block_maps[level_index], child_front, 0, keepdims=False
            )
            upper = extend_add(schur, blocks)
            partial_value = upper[:, :PIV]
            trailing = upper[PIV:, PIV:]
        start = position * row_count
        current = lax.dynamic_slice_in_dim(partial_value, start, row_count, 0)
        partial_value = lax.dynamic_update_slice_in_dim(
            partial_value, current + panel_rows, start, 0
        )
        assembled = group_total(partial_value, level_index)
        inverse = inverse_factor(assembled[:PIV])
        column_count = PIV // group_devices
        picked = lax.dynamic_slice_in_dim(inverse, position * column_count, column_count, 0)
        columns = exact_dot(assembled[PIV:], picked.T)
        schur = trailing - exact_dot(columns, columns.T)
    sub_rows = UPD // (8 * row_devices)
    grouped = jnp.swapaxes(schur.reshape(8, row_devices, sub_rows, UPD), 0, 1)
    shared = lax.psum_scatter(grouped, "row", scatter_dimension=0, tiled=True)
    current = shared[0]
    for bit_number in (2, 1, 0):
        half_count = current.shape[0] // 2
        upper_side = leaf_index // 2**bit_number % 2
        lower_half = current[:half_count]
        upper_half = current[half_count:]
        kept_half = jnp.where(upper_side == 1, upper_half, lower_half)
        given_half = jnp.where(upper_side == 1, lower_half, upper_half)
        current = kept_half + partner(given_half, "leaf", bit_number)
    return current.reshape(sub_rows, UPD)


def solution(mesh):
    placed = (
        P(("leaf", "row"), None),
        P(("leaf", "row"), None),
        P(("leaf", "row"), None),
        P(("leaf", "row"), None),
        P(),
        P(),
        P(),
    )
    return jax.shard_map(
        body, mesh=mesh, in_specs=placed, out_specs=P(("leaf", "row"), None), check_vma=False
    )
```

profile of v0, /device:TPU:6, one launch (start us, length us, event | category | flops | bytes accessed | tf_op | source)
XLA Modules:
  0.0 1516.8 jit_solution(17720124293818263964)
XLA Ops:
  16.1 68.2 %all-reduce.11.cloned.1.call-done = f32[1536,512]{0,1:T(8,128)} async-done(((f32[1536,512]{0,1:T(8,128)}), f32[1536,512]{0,1:T(8,128)}) %all-reduce.11.cloned.1.call-update) | async-done | bytes 3145744 | tf_op jit(solution)/shard_map/psum | solution.py:86
  86.1 11.7 cholesky.254
  112.5 11.7 cholesky.265
  136.7 11.7 cholesky.276
  162.2 11.9 cholesky.287
  229.3 68.9 %all-reduce.13.cloned.1.call-done = f32[1536,512]{0,1:T(8,128)} async-done(((f32[1536,512]{0,1:T(8,128)}), f32[1536,512]{0,1:T(8,128)}) %all-reduce.13.cloned.1.call-update) | async-done | bytes 3145744 | tf_op jit(solution)/shard_map/psum | solution.py:86
  302.2 66.6 %collective-permute-done = f32[1536,512]{0,1:T(8,128)} collective-permute-done((f32[1536,512]{0,1:T(8,128)}, f32[1536,512]{0,1:T(8,128)}, u32[]{:S(2)}, u32[]{:S(2)}) %collective-permute-start) | collective-permute-done | bytes 3145760 | tf_op jit(solution)/shard_map/ppermute | solution.py:21
  372.3 11.7 cholesky.298
  399.1 11.7 cholesky.309
  429.6 13.2 cholesky.320
  446.6 11.3 custom-call.26
  474.9 13.3 cholesky.331
  560.3 67.7 %all-reduce.15.cloned.1.call-done = f32[1536,512]{0,1:T(8,128)} async-done(((f32[1536,512]{0,1:T(8,128)}), f32[1536,512]{0,1:T(8,128)}) %all-reduce.15.cloned.1.call-update) | async-done | bytes 3145744 | tf_op jit(solution)/shard_map/psum | solution.py:86
  629.6 68.9 %collective-permute-done.1 = f32[1536,512]{0,1:T(8,128)S(1)} collective-permute-done((f32[1536,512]{0,1:T(8,128)}, f32[1536,512]{0,1:T(8,128)S(1)}, u32[]{:S(2)}, u32[]{:S(2)}) %collective-permute-start.1) | collective-permute-done | bytes 3145760 | tf_op jit(solution)/shard_map/ppermute | solution.py:21
  706.0 67.5 %collective-permute-done.2 = f32[1536,512]{0,1:T(8,128)} collective-permute-done((f32[1536,512]{0,1:T(8,128)S(1)}, f32[1536,512]{0,1:T(8,128)}, u32[]{:S(2)}, u32[]{:S(2)}) %collective-permute-start.2) | collective-permute-done | bytes 3145760 | tf_op jit(solution)/shard_map/ppermute | solution.py:21
  778.7 11.7 cholesky.342
  807.6 11.7 cholesky.353
  844.0 13.2 cholesky.364
  860.9 11.3 custom-call.30
  884.2 13.6 cholesky.375
  901.4 11.3 custom-call.31
  967.8 68.2 %all-reduce.17.cloned.1.call-done = f32[1536,512]{0,1:T(8,128)} async-done(((f32[1536,512]{0,1:T(8,128)}), f32[1536,512]{0,1:T(8,128)}) %all-reduce.17.cloned.1.call-update) | async-done | bytes 3145744 | tf_op jit(solution)/shard_map/psum | solution.py:86
  1037.6 68.9 %collective-permute-done.3 = f32[1536,512]{0,1:T(8,128)S(1)} collective-permute-done((f32[1536,512]{0,1:T(8,128)}, f32[1536,512]{0,1:T(8,128)S(1)}, u32[]{:S(2)}, u32[]{:S(2)}) %collective-permute-start.3) | collective-permute-done | bytes 3145760 | tf_op jit(solution)/shard_map/ppermute | solution.py:21
  1112.3 68.9 %collective-permute-done.4 = f32[1536,512]{0,1:T(8,128)S(1)} collective-permute-done((f32[1536,512]{0,1:T(8,128)S(1)}, f32[1536,512]{0,1:T(8,128)S(1)}, u32[]{:S(2)}, u32[]{:S(2)}) %collective-permute-start.4) | collective-permute-done | bytes 3145760 | tf_op jit(solution)/shard_map/ppermute | solution.py:21
  1183.8 68.4 %collective-permute-done.5 = f32[1536,512]{0,1:T(8,128)} collective-permute-done((f32[1536,512]{0,1:T(8,128)S(1)}, f32[1536,512]{0,1:T(8,128)}, u32[]{:S(2)}, u32[]{:S(2)}) %collective-permute-start.5) | collective-permute-done | bytes 3145760 | tf_op jit(solution)/shard_map/ppermute | solution.py:21
  1257.4 11.7 cholesky.386
  1286.3 11.7 cholesky.397
  1322.7 13.2 cholesky.408
  1339.6 11.3 custom-call.34
  1363.0 13.3 cholesky.419
  1380.0 11.3 custom-call.35
  1413.6 70.3 %all-reduce.19.cloned.1.call-done = f32[8,8,16,1024]{3,2,0,1:T(8,128)} async-done(((f32[8,8,16,1024]{3,2,0,1:T(8,128)}), f32[8,8,16,1024]{3,2,0,1:T(8,128)}) %all-reduce.19.cloned.1.call-update) | async-done | bytes 4194320
  (358 shorter events, 496.0 us)
Async XLA Ops:
  6.5 9.4 copy-start
  6.5 77.8 %all-reduce.11.cloned.1.call-start = ((), (), s32[]{:S(2)}) async-start(), calls=%async_computation | async-start | bytes 6291456 | tf_op jit(solution)/shard_map/psum | solution.py:86
  13.1 1.7 copy-start.5
  14.8 283.5 %all-reduce.13.cloned.1.call-start = ((), (), s32[]{:S(2)}) async-start(), calls=%async_computation.1 | async-start | bytes 6291456 | tf_op jit(solution)/shard_map/psum | solution.py:86
  188.3 7.7 copy-start.22
  227.6 1.7 copy-start.2
  229.3 398.7 %all-reduce.15.cloned.1.call-start = ((), (), s32[]{:S(2)}) async-start(), calls=%async_computation.2 | async-start | bytes 6291456 | tf_op jit(solution)/shard_map/psum | solution.py:86
  298.3 70.5 %collective-permute-start = (f32[1536,512]{0,1:T(8,128)}, f32[1536,512]{0,1:T(8,128)}, u32[]{:S(2)}, u32[]{:S(2)}) collective-permute-start(f32[1536,512]{0,1:T(8,128)} %all-reduce.13.cloned.1.call-done), channel_id=1, source_target_pairs={{0,8},{8,0},{16,24},{24,16},{32,40},{40,32},{48,56},{56,48},{64,72... | collective-permute-start | bytes 9437192 | tf_op jit(solution)/shard_map/ppermute | solution.py:21
  552.6 2.4 copy-start.26
  558.6 1.7 copy-start.3
  560.3 144.2 %copy-start.28 = (f32[24,512]{1,0:T(8,128)S(1)}, f32[24,512]{1,0:T(8,128)}, u32[]{:S(2)}) copy-start(f32[24,512]{1,0:T(8,128)} %param.37) | copy-start | bytes 147460
  560.3 475.8 %all-reduce.17.cloned.1.call-start = ((), (), s32[]{:S(2)}) async-start(), calls=%async_computation.3 | async-start | bytes 6291456 | tf_op jit(solution)/shard_map/psum | solution.py:86
  628.0 70.4 %collective-permute-start.1 = (f32[1536,512]{0,1:T(8,128)}, f32[1536,512]{0,1:T(8,128)S(1)}, u32[]{:S(2)}, u32[]{:S(2)}) collective-permute-start(f32[1536,512]{0,1:T(8,128)} %all-reduce.15.cloned.1.call-done), channel_id=1, source_target_pairs={{0,8},{8,0},{16,24},{24,16},{32,40},{40,32},{48,56},{56,48},{64,72... | collective-permute-start | bytes 9437192 | tf_op jit(solution)/shard_map/ppermute | solution.py:21
  701.0 72.5 %collective-permute-start.2 = (f32[1536,512]{0,1:T(8,128)S(1)}, f32[1536,512]{0,1:T(8,128)}, u32[]{:S(2)}, u32[]{:S(2)}) collective-permute-start(f32[1536,512]{0,1:T(8,128)S(1)} %add.230), channel_id=1, source_target_pairs={{0,16},{16,0},{8,24},{24,8},{32,48},{48,32},{40,56},{56,40},{64,80... | collective-permute-start | bytes 9437192 | tf_op jit(solution)/shard_map/ppermute | solution.py:21
  806.5 119.5 %copy-start.9 = (f32[1536,512]{0,1:T(8,128)S(1)}, f32[1536,512]{0,1:T(8,128)}, u32[]{:S(2)}) copy-start(f32[1536,512]{0,1:T(8,128)} %copy-done.8) | copy-start | bytes 9437188
  834.4 5.9 copy-start.23
  873.2 2.9 copy-start.14
  874.4 1.8 copy-start.17
  960.1 2.4 copy-start.27
  966.1 1.7 copy-start.4
  967.8 516.2 %all-reduce.19.cloned.1.call-start = ((), (), s32[]{:S(2)}) async-start(), calls=%async_computation.4 | async-start | bytes 8388608
  1036.0 70.4 %collective-permute-start.3 = (f32[1536,512]{0,1:T(8,128)}, f32[1536,512]{0,1:T(8,128)S(1)}, u32[]{:S(2)}, u32[]{:S(2)}) collective-permute-start(f32[1536,512]{0,1:T(8,128)} %all-reduce.17.cloned.1.call-done), channel_id=1, source_target_pairs={{0,8},{8,0},{16,24},{24,16},{32,40},{40,32},{48,56},{56,48},{64,72... | collective-permute-start | bytes 9437192 | tf_op jit(solution)/shard_map/ppermute | solution.py:21
  1109.0 72.2 %collective-permute-start.4 = (f32[1536,512]{0,1:T(8,128)S(1)}, f32[1536,512]{0,1:T(8,128)S(1)}, u32[]{:S(2)}, u32[]{:S(2)}) collective-permute-start(f32[1536,512]{0,1:T(8,128)S(1)} %add.241), channel_id=1, source_target_pairs={{0,16},{16,0},{8,24},{24,8},{32,48},{48,32},{40,56},{56,40},{64,80... | collective-permute-start | bytes 9437192 | tf_op jit(solution)/shard_map/ppermute | solution.py:21
  1181.8 70.4 %collective-permute-start.5 = (f32[1536,512]{0,1:T(8,128)S(1)}, f32[1536,512]{0,1:T(8,128)}, u32[]{:S(2)}, u32[]{:S(2)}) collective-permute-start(f32[1536,512]{0,1:T(8,128)S(1)} %add.242), channel_id=1, source_target_pairs={{0,32},{32,0},{8,40},{40,8},{16,48},{48,16},{24,56},{56,24},{64,96... | collective-permute-start | bytes 9437192 | tf_op jit(solution)/shard_map/ppermute | solution.py:21
  1285.2 119.3 %copy-start.7 = (f32[1536,512]{0,1:T(8,128)S(1)}, f32[1536,512]{0,1:T(8,128)}, u32[]{:S(2)}) copy-start(f32[1536,512]{0,1:T(8,128)} %copy-done.6) | copy-start | bytes 9437188
  1313.1 5.9 copy-start.24
  1352.0 2.9 copy-start.15
  1353.2 1.8 copy-start.18
  1412.4 97.7 %copy-start.1 = (s32[16,8]{0,1:T(8,128)S(1)}, s32[16,8]{0,1:T(8,128)}, u32[]{:S(2)}) copy-start(s32[16,8]{0,1:T(8,128)} %param.38) | copy-start | bytes 1540
  1487.3 8.1 collective-permute-start.6
  1497.1 7.9 collective-permute-start.7
  1505.1 4.3 collective-permute-start.8
  (12 other events, 11.2 us)
Sparse Core Ops, SparseCore 0:
  14.9 69.3 all-reduce.10
  229.4 68.8 all-reduce.12
  560.4 67.5 all-reduce.14
  967.9 68.1 all-reduce.16
  1412.5 71.3 all-reduce.18
where the time goes:
time: 1530 us; the launch traced here: 1520 us
  waiting for transfers between devices  767 us (50%)
  other arithmetic  434 us (28%)
  matrix products  171 us (11%)
  local copies, waits for them, and re-layouts  110 us (7%)
  starting transfers between devices  19.9 us (1%)
    ppermute x9, waiting for transfers between devices, partner(): return lax.ppermute(block, axis, route)  423 us
    psum x4, waiting for transfers between devices, group_total(): assembled = lax.psum(partial_value, 'row')  273 us
    another operation x48, other arithmetic, inverse_factor(): jnp.linalg.cholesky(remaining[offset:offset + BLOCK, offset:offset + BLOCK])  213 us
    another operation x32, other arithmetic, inverse_factor(): jax.scipy.linalg.solve_triangular(diag_factor, identity, lower=True)  186 us
    dot_general x96, matrix products, exact_dot(): jnp.dot(left, right, precision=exact_mode, preferred_element_type=jnp.flo...  122 us
    unnamed x6, waiting for transfers between devices  70.4 us
    unnamed x74, local copies, waits for them, and re-layouts  57.9 us
  transfers between devices with their start and end apart: 14, of which 14 were waited for; matrix products, arithmetic and copies ran while one was open for 0% of the time, Pallas kernels for 0%

commit v1 on v0

v1 whole, which is shorter than its diff:
```python
import functools

import jax
import jax.numpy as jnp
from jax import lax
from jax.experimental import pallas as pl
from jax.experimental.pallas import tpu as pltpu
from jax.sharding import PartitionSpec as P

BLOCK = 128
PIV = 512
UPD = 1024
FRONT = PIV + UPD
SUB = 8
WIDTH = 16
PIV_BLOCKS = PIV // BLOCK
UPD_BLOCKS = UPD // BLOCK
PIECE_ROWS = 192
LOWER = [(p, q) for p in range(PIV_BLOCKS) for q in range(p + 1)]
PACKED = [(a, b) for a in range(UPD_BLOCKS) for b in range(a + 1)]
HALF_ROWS = len(LOWER) * BLOCK // 2
SHARE_ROWS = len(PACKED) * BLOCK // 8
VMEM_BYTES = 56 * 1024 * 1024

f32 = jnp.float32
bf16 = jnp.bfloat16


def split(x):
    high = x.astype(bf16)
    return high, (x - high.astype(f32)).astype(bf16)


def dot3(left, right, transposed=False):
    dims = (((1,), (1 if transposed else 0,)), ((), ()))
    dot = functools.partial(lax.dot_general, dimension_numbers=dims, preferred_element_type=f32)
    return dot(left[0], right[0]) + (dot(left[0], right[1]) + dot(left[1], right[0]))


def reciprocal(x):
    r = pltpu.reciprocal(x, approx=True)
    return r * (2.0 - x * r)


def inverse_block(rows):
    count = len(rows)
    parts = WIDTH // SUB
    shape = (SUB, BLOCK)
    lane = lax.broadcasted_iota(jnp.int32, shape, 1)
    sub = lax.broadcasted_iota(jnp.int32, shape, 0)
    rows = list(rows)

    def row_of(x, t):
        return jnp.broadcast_to(x[t : t + 1, :], shape)

    def lane_of(x, l):
        return jnp.broadcast_to(x[:, l : l + 1], shape)

    for g in range(count // parts):
        base = g * WIDTH
        inside = (lane >= base) & (lane < base + WIDTH)
        cols = [[lane_of(rows[parts * g + h], base + i) for i in range(WIDTH)] for h in range(parts)]
        strip = [
            jnp.where(inside, jnp.where(lane == base + h * SUB + sub, 1.0, 0.0), rows[parts * g + h])
            for h in range(parts)
        ]
        for i in range(0, WIDTH, 2):
            h, t = i // SUB, i % SUB
            a, b = row_of(cols[h][i], t), row_of(cols[h][i + 1], t)
            c, d = row_of(cols[h][i], t + 1), row_of(cols[h][i + 1], t + 1)
            r = reciprocal(a * d - b * c)
            ar, br, cr, dr = a * r, b * r, c * r, d * r

            def eliminate(col):
                x, y = row_of(col[h], t), row_of(col[h], t + 1)
                f, e = dr * x - br * y, ar * y - cr * x
                out = [col[k] - (cols[k][i] * f + cols[k][i + 1] * e) for k in range(parts)]
                out[h] = jnp.where(sub == t, f, jnp.where(sub == t + 1, e, out[h]))
                return out

            for j in range(i + 2, WIDTH):
                done = eliminate([cols[k][j] for k in range(parts)])
                for k in range(parts):
                    cols[k][j] = done[k]
            strip = eliminate(strip)
        near = [v for v in range(parts * (g + 1), parts * (g + 2)) if v < count]
        far = [v for v in range(count) if v not in near and v // parts != g]
        wide = [row_of(strip[i // SUB], i % SUB) for i in range(WIDTH)] if near else []
        for v in near:
            terms = [lane_of(rows[v], base + i) * wide[i] for i in range(WIDTH)]
            while len(terms) > 1:
                terms = [terms[k] + terms[k + 1] for k in range(0, len(terms), 2)]
            rows[v] = jnp.where(inside, 0.0, rows[v]) - terms[0]
        above = [jnp.zeros((base, BLOCK), f32)] if base else []
        below = [jnp.zeros((BLOCK - base - WIDTH, BLOCK), f32)] if base + WIDTH < BLOCK else []
        padded = jnp.concatenate(above + strip + below, 0)
        update = dot3(split(jnp.concatenate([rows[v] for v in far], 0)), split(padded))
        for k, v in enumerate(far):
            rows[v] = jnp.where(inside, 0.0, rows[v]) - update[k * SUB : (k + 1) * SUB]
        for h in range(parts):
            rows[parts * g + h] = strip[h]
    return jnp.concatenate(rows, 0)


def invert(ref):
    for j in range(PIV_BLOCKS):
        js = slice(j * BLOCK, (j + 1) * BLOCK)
        inverse = inverse_block(
            [ref[j * BLOCK + v * SUB : j * BLOCK + (v + 1) * SUB, js] for v in range(BLOCK // SUB)]
        )
        others = list(range(j + 1, PIV_BLOCKS)) + list(range(j))
        inverse_s = split(inverse)
        left = {i: split(ref[i * BLOCK : (i + 1) * BLOCK, js]) for i in others}
        top = {k: dot3(inverse_s, split(ref[js, k * BLOCK : (k + 1) * BLOCK])) for k in others}
        top_s = {k: split(top[k]) for k in others}
        for i in others:
            rows = slice(i * BLOCK, (i + 1) * BLOCK)
            for k in others:
                columns = slice(k * BLOCK, (k + 1) * BLOCK)
                ref[rows, columns] = ref[rows, columns] - dot3(left[i], top_s[k])
            ref[rows, js] = -dot3(left[i], inverse_s)
        for k in others:
            ref[js, k * BLOCK : (k + 1) * BLOCK] = top[k]
        ref[js, js] = inverse


def rows_at(index, count):
    return pl.ds(pl.multiple_of(index * count, SUB), count)


def place_panel(level, place, pieces, whole):
    count = PIECE_ROWS >> level
    x, core, leaf = place[0], place[1], place[2]
    for k in range(4):
        for c in range(2):
            for t in range(1 << level):
                owner = (leaf ^ t) * 8 + (x ^ k) * 2 + (core ^ c)
                whole[rows_at(owner, count), :] = pieces[k * 2 + c][t * count : (t + 1) * count, :]


def place_kernel(level, place, *refs):
    pieces, (pivot, below), (whole,) = refs[:8], refs[8:10], refs[10:]
    place_panel(level, place, pieces, whole)
    pivot[...] = whole[:PIV, :]
    below[...] = whole[PIV:, :]


def first_factor_kernel(place, *refs):
    pieces, (inverse, below), (whole,) = refs[:8], refs[8:10], refs[10:]
    place_panel(0, place, pieces, whole)
    inverse[...] = whole[:PIV, :]
    below[...] = whole[PIV:, :]
    invert(inverse)


def factor_kernel(place, pivot, mine, same, other, inverse, theirs):
    core = place[1]
    theirs[rows_at(core, HALF_ROWS), :] = same[...]
    theirs[rows_at(1 - core, HALF_ROWS), :] = other[...]
    for n, (p, q) in enumerate(LOWER):
        ps, qs = slice(p * BLOCK, (p + 1) * BLOCK), slice(q * BLOCK, (q + 1) * BLOCK)
        ns = slice(n * BLOCK, (n + 1) * BLOCK)
        total = pivot[ps, qs] + (mine[ns, :] + theirs[ns, :])
        inverse[ps, qs] = total
        if p != q:
            inverse[qs, ps] = total.T
    invert(inverse)


def block_of(ref, index_a, index_b):
    present = (index_a >= 0) & (index_b >= 0)
    spot = jnp.maximum(index_a, 0) * UPD_BLOCKS + jnp.maximum(index_b, 0)
    return jnp.where(present, ref[rows_at(spot, BLOCK), :], 0.0)


def extended(tables, level, mine, theirs, p, q):
    base = (level - 1) * 24
    own = block_of(mine, tables[base + p], tables[base + q])
    return own + block_of(theirs, tables[base + 12 + p], tables[base + 12 + q])


def mirror_shares(place, shares, packed, theirs):
    x, core = place[0], place[1]
    for k in range(4):
        for c in range(2):
            owner = (x ^ k) * 2 + (core ^ c)
            packed[rows_at(owner, SHARE_ROWS), :] = shares[k * 2 + c][...]
    for n, (a, b) in enumerate(PACKED):
        block = packed[n * BLOCK : (n + 1) * BLOCK, :]
        spot = (a * UPD_BLOCKS + b) * BLOCK
        theirs[spot : spot + BLOCK, :] = block
        if a != b:
            spot = (b * UPD_BLOCKS + a) * BLOCK
            theirs[spot : spot + BLOCK, :] = block.T


def assemble_below(level, tables, below, mine, theirs, columns):
    for u in range(UPD_BLOCKS):
        us = slice(u * BLOCK, (u + 1) * BLOCK)
        for q in range(PIV_BLOCKS):
            qs = slice(q * BLOCK, (q + 1) * BLOCK)
            columns[us, qs] = below[us, qs] + extended(tables, level, mine, theirs, PIV_BLOCKS + u, q)


def next_pivot(level, place, tables, mine, theirs, columns, weighted, parent, half):
    base = level * 24
    for n, (p, q) in enumerate(LOWER):
        a, b = tables[base + p], tables[base + q]
        a0, b0 = jnp.maximum(a, 0), jnp.maximum(b, 0)
        block = -dot3(
            split(weighted[rows_at(a0, BLOCK), :]), split(columns[rows_at(b0, BLOCK), :]), transposed=True
        )
        if level:
            block = block + extended(tables, level, mine, theirs, PIV_BLOCKS + a0, PIV_BLOCKS + b0)
        parent[n * BLOCK : (n + 1) * BLOCK, :] = jnp.where((a >= 0) & (b >= 0), block, 0.0)
    half[...] = parent[rows_at(place[1], HALF_ROWS), :]


def weigh(columns, inverse, weighted):
    inverse_s = split(inverse[...])
    for u in range(0, UPD, 256):
        weighted[u : u + 256, :] = dot3(split(columns[u : u + 256, :]), inverse_s)


def first_columns_kernel(place, tables, inverse, below, weighted, parent, half):
    weigh(below, inverse, weighted)
    next_pivot(0, place, tables, None, None, below, weighted, parent, half)


def columns_kernel(level, place, tables, inverse, below, mine, *refs):
    shares, (columns, weighted, parent, half, theirs), (packed,) = refs[:8], refs[8:13], refs[13:]
    mirror_shares(place, shares, packed, theirs)
    assemble_below(level, tables, below, mine, theirs, columns)
    weigh(columns, inverse, weighted)
    next_pivot(level, place, tables, mine, theirs, columns, weighted, parent, half)


def update_body(level, place, tables, columns, weighted, mine, theirs, update, share, packed):
    right = split(columns[...])
    for a in range(UPD_BLOCKS):
        left = split(weighted[a * BLOCK : (a + 1) * BLOCK, :])
        strip = dot3(left, right, transposed=True)
        for b in range(UPD_BLOCKS):
            block = -strip[:, b * BLOCK : (b + 1) * BLOCK]
            if level:
                block = block + extended(tables, level, mine, theirs, PIV_BLOCKS + a, PIV_BLOCKS + b)
            spot = (a * UPD_BLOCKS + b) * BLOCK
            update[spot : spot + BLOCK, :] = block
            if b <= a:
                n = PACKED.index((a, b))
                packed[n * BLOCK : (n + 1) * BLOCK, :] = block
    share[...] = packed[rows_at(place[0] * 2 + place[1], SHARE_ROWS), :]


def first_update_kernel(place, tables, columns, weighted, update, share, packed):
    update_body(0, place, tables, columns, weighted, None, None, update, share, packed)


def update_kernel(level, place, tables, columns, weighted, mine, theirs, update, share, packed):
    update_body(level, place, tables, columns, weighted, mine, theirs, update, share, packed)


def last_kernel(level, place, tables, inverse, below, mine, *refs):
    shares, (out,), (packed, theirs, columns) = refs[:8], refs[8:9], refs[9:]
    mirror_shares(place, shares, packed, theirs)
    assemble_below(level, tables, below, mine, theirs, columns)
    count = out.shape[0]
    position = place[2] * 8 + place[0] * 2 + place[1]
    per_block = BLOCK // count
    block_row, inner = position // per_block, position % per_block
    left = split(columns[rows_at(position, count), :])
    weighted = split(dot3(left, split(inverse[...])))
    strip = dot3(weighted, split(columns[...]), transposed=True)
    base = (level - 1) * 24

    def part(ref, index_a, index_b):
        present = (index_a >= 0) & (index_b >= 0)
        spot = (jnp.maximum(index_a, 0) * UPD_BLOCKS + jnp.maximum(index_b, 0)) * per_block + inner
        return jnp.where(present, ref[rows_at(spot, count), :], 0.0)

    for v in range(UPD_BLOCKS):
        mine_a, mine_b = tables[base + PIV_BLOCKS + block_row], tables[base + PIV_BLOCKS + v]
        their_a, their_b = tables[base + 12 + PIV_BLOCKS + block_row], tables[base + 12 + PIV_BLOCKS + v]
        vs = slice(v * BLOCK, (v + 1) * BLOCK)
        out[:, vs] = part(mine, mine_a, mine_b) + part(theirs, their_a, their_b) - strip[:, vs]


SMEM = pl.BlockSpec(memory_space=pltpu.SMEM)
VMEM = pl.BlockSpec(memory_space=pltpu.VMEM)


def call(kernel, name, scalars, arrays, outs, scratch, micros):
    shapes = [jax.ShapeDtypeStruct(shape, f32) for shape in outs]
    return pl.pallas_call(
        kernel,
        out_shape=shapes,
        in_specs=[SMEM] * len(scalars) + [VMEM] * len(arrays),
        out_specs=[VMEM] * len(outs),
        scratch_shapes=[pltpu.VMEM(shape, f32) for shape in scratch],
        compiler_params=pltpu.CompilerParams(vmem_limit_bytes=VMEM_BYTES),
        cost_estimate=pl.CostEstimate(flops=int(micros * 1.1e9), bytes_accessed=4096, transcendentals=0),
        name=name,
    )(*scalars, *arrays)


def flip(value, axis, mask):
    count = lax.axis_size(axis)
    return lax.ppermute(value, axis, [(i, i ^ mask) for i in range(count)])


def gather_row(value):
    chips = [value] + [flip(value, "row", 2 * k) for k in (1, 2, 3)]
    pieces = []
    for one in chips:
        pieces += [one, flip(one, "row", 1)]
    return pieces


def gather_panel(value, level):
    for bit in range(level):
        value = jnp.concatenate([value, flip(value, "leaf", 1 << bit)], axis=0)
    return gather_row(value)


def after(value, *others):
    return lax.optimization_barrier((value, *others))[0]


def inverse_map(blocks):
    spots = jnp.arange(FRONT // BLOCK, dtype=jnp.int32)
    order = jnp.arange(1, UPD_BLOCKS + 1, dtype=jnp.int32)
    return jnp.sum(jnp.where(blocks[:, None] == spots[None, :], order[:, None], 0), axis=0) - 1


def body(panel0, panel1, panel2, panel3, maps1, maps2, maps3):
    panels = (panel0, panel1, panel2, panel3)
    leaf = lax.axis_index("leaf")
    row = lax.axis_index("row")
    rows = []
    for level, maps in ((1, maps1), (2, maps2), (3, maps3)):
        child = leaf >> (level - 1)
        for front in (child, child ^ 1):
            rows.append(inverse_map(lax.dynamic_index_in_dim(maps, front, 0, keepdims=False)))
    tables = jnp.concatenate(rows)
    places = [jnp.stack([row // 2, row % 2, leaf % (1 << level)]).astype(jnp.int32) for level in range(4)]

    gathered = {0: gather_panel(panels[0], 0)}
    gathered[1] = gather_panel(after(panels[1], *gathered[0][1::2]), 1)
    gathered[2] = gather_panel(after(panels[2], *gathered[1][1::2]), 2)
    gathered[3] = gather_panel(after(panels[3], *gathered[2][1::2]), 3)

    inverse, below = call(
        first_factor_kernel, "factor0", [places[0]], gathered[0],
        [(PIV, PIV), (UPD, PIV)], [(FRONT, PIV)], 18,
    )
    weighted, parent, half = call(
        first_columns_kernel, "columns0", [places[0], tables], [inverse, below],
        [(UPD, PIV), (2 * HALF_ROWS, BLOCK), (HALF_ROWS, BLOCK)], [], 6,
    )
    update, share = call(
        first_update_kernel, "update0", [places[0], tables], [below, weighted],
        [(UPD_BLOCKS * UPD, BLOCK), (SHARE_ROWS, BLOCK)], [(len(PACKED) * BLOCK, BLOCK)], 6,
    )
    for level in (1, 2, 3):
        bit = 1 << (level - 1)
        same = flip(half, "leaf", bit)
        other = flip(same, "row", 1)
        shares = gather_row(flip(share, "leaf", bit))
        pivot, below = call(
            functools.partial(place_kernel, level), f"place{level}", [places[level]], gathered[level],
            [(PIV, PIV), (UPD, PIV)], [(FRONT, PIV)], 3,
        )
        inverse = call(
            factor_kernel, f"factor{level}", [places[level]], [pivot, parent, same, other],
            [(PIV, PIV)], [(2 * HALF_ROWS, BLOCK)], 18,
        )[0]
        if level == 3:
            return call(
                functools.partial(last_kernel, level), "last", [places[level], tables],
                [inverse, below, update, *shares], [(UPD // 64, UPD)],
                [(len(PACKED) * BLOCK, BLOCK), (UPD_BLOCKS * UPD, BLOCK), (UPD, PIV)], 8,
            )[0]
        columns, weighted, parent, half, theirs = call(
            functools.partial(columns_kernel, level), f"columns{level}", [places[level], tables],
            [inverse, below, update, *shares],
            [(UPD, PIV), (UPD, PIV), (2 * HALF_ROWS, BLOCK), (HALF_ROWS, BLOCK), (UPD_BLOCKS * UPD, BLOCK)],
            [(len(PACKED) * BLOCK, BLOCK)], 10,
        )
        update, share = call(
            functools.partial(update_kernel, level), f"update{level}", [places[level], tables],
            [columns, weighted, update, theirs],
            [(UPD_BLOCKS * UPD, BLOCK), (SHARE_ROWS, BLOCK)], [(len(PACKED) * BLOCK, BLOCK)], 8,
        )


def solution(mesh):
    panel = P(("leaf", "row"), None)
    return jax.shard_map(
        body, mesh=mesh, in_specs=(panel,) * 4 + (P(),) * 3, out_specs=panel, check_vma=False
    )
```

time: 1530 us -> 368 us (0.24)
  waiting for transfers between devices: 767 us -> 132 us
  other arithmetic: 434 us -> 1.48 us
  matrix products: 171 us -> 0 us
  Pallas kernels: 0 us -> 159 us
  local copies, waits for them, and re-layouts: 110 us -> 9.07 us
  starting transfers between devices: 19.9 us -> 61.5 us
    another operation x80 -> x2, other arithmetic: 399 us -> 1.33 us  [body(): jnp.stack([row // 2, row % 2, leaf % (1 << level)]).astype(jnp.int32)]
    ppermute x9 -> x64, waiting for transfers between devices: 423 us -> 132 us  [flip(): return lax.ppermute(value, axis, [(i, i ^ mask) for i in range(count)])]
    psum x4 -> x0, waiting for transfers between devices: 273 us -> none  [group_total(): assembled = lax.psum(partial_value, 'row')]
    dot_general x102 -> x0, matrix products: 160 us -> none  [the longest x96 122 us: exact_dot(): jnp.dot(left, right, precision=exact_mode, preferred_element_type=jnp.flo...]
    pallas_call x0 -> x14, Pallas kernels: none -> 159 us  [call(): pl.pallas_call(kernel, out_shape=shapes, in_specs=[SMEM] * len(scalars) +...]
    unnamed x6 -> x0, waiting for transfers between devices: 70.4 us -> none
    unnamed x74 -> x132, local copies, waits for them, and re-layouts: 57.9 us -> 5.89 us
    ppermute x9 -> x64, starting transfers between devices: 19.7 us -> 61.5 us  [flip(): return lax.ppermute(value, axis, [(i, i ^ mask) for i in range(count)])]
  transfers between devices with their start and end apart: 14 -> 64, of which waited for: 14 -> 20; matrix products, arithmetic and copies ran while one was open for 0% -> 1% of each run, Pallas kernels for 0% -> 42%
where the time goes in v1:
time: 368 us; the launch traced here: 364 us
  Pallas kernels  159 us (43%)
  waiting for transfers between devices  132 us (36%)
  starting transfers between devices  61.5 us (17%)
  local copies, waits for them, and re-layouts  9.07 us (2%)
    pallas_call x14, Pallas kernels, call(): pl.pallas_call(kernel, out_shape=shapes, in_specs=[SMEM] * len(scalars) +...  159 us
    ppermute x64, waiting for transfers between devices, flip(): return lax.ppermute(value, axis, [(i, i ^ mask) for i in range(count)])  132 us
    ppermute x64, starting transfers between devices, flip(): return lax.ppermute(value, axis, [(i, i ^ mask) for i in range(count)])  61.5 us
  transfers between devices with their start and end apart: 64, of which 20 were waited for; matrix products, arithmetic and copies ran while one was open for 1% of the time, Pallas kernels for 42%

profile of v1, /device:TPU:6, one launch (start us, length us, event | category | flops | bytes accessed | tf_op | source)
XLA Modules:
  0.0 364.3 jit_solution(16265339525465051476)
XLA Ops:
  7.3 4.9 %collective-permute-done.1.refs_2_ = f32[192,512]{1,0:T(8,128)S(1)} collective-permute-done((f32[192,512]{1,0:T(8,128)}, f32[192,512]{1,0:T(8,128)S(1)}, u32[]{:S(2)}, u32[]{:S(2)}) %collective-permute-start.1) | collective-permute-done | bytes 393248 | tf_op jit(solution)/shard_map/ppermute | solution.py:308
  12.2 7.0 %collective-permute-done.3.refs_4_ = f32[192,512]{1,0:T(8,128)S(1)} collective-permute-done((f32[192,512]{1,0:T(8,128)}, f32[192,512]{1,0:T(8,128)S(1)}, u32[]{:S(2)}, u32[]{:S(2)}) %collective-permute-start.3) | collective-permute-done | bytes 393248 | tf_op jit(solution)/shard_map/ppermute | solution.py:308
  25.9 18.4 %factor0.1 = (f32[512,512]{1,0:T(8,128)}, f32[1024,512]{1,0:T(8,128)}) custom-call(s32[3]{0:T(128)} %get-tuple-element.73.place, f32[192,512]{1,0:T(8,128)} %refs_0_.1, f32[192,512]{1,0:T(8,128)} %copy-done.9, f32[192,512]{1,0:T(8,128)} %copy-done.6, f32[192,512]{1,0:T(8,128)} %copy-done.17, f32[192,512]{1,0:T(8,128)} %copy-done.7, f32[192,512]{1,0:T(8,128)} %copy-done.18, ...), custom_call_target="tpu_custom_call" | custom-call | flops 19800000512 | bytes 4096 | tf_op jit(solution)/shard_map/factor0/pallas_call | solution.py:294
  44.4 6.3 %columns0.1 = (f32[1024,512]{1,0:T(8,128)}, f32[1280,128]{1,0:T(8,128)}, f32[640,128]{1,0:T(8,128)}) custom-call(s32[3]{0:T(128)} %get-tuple-element.73.place, s32[72]{0:T(128)} %concatenate.24.tables, f32[512,512]{1,0:T(8,128)} %get-tuple-element.41.inverse, f32[1024,512]{1,0:T(8,128)} %get-tuple-element.42.below.columns), custom_call_target="tpu_custom_call" | custom-call | flops 6600000000 | bytes 4096 | tf_op jit(solution)/shard_map/columns0/pallas_call | solution.py:294
  50.6 12.5 %update0.1 = (f32[8192,128]{1,0:T(8,128)}, f32[576,128]{1,0:T(8,128)}) custom-call(s32[3]{0:T(128)} %get-tuple-element.73.place, s32[72]{0:T(128)} %concatenate.24.tables, f32[1024,512]{1,0:T(8,128)} %get-tuple-element.42.below.columns, f32[1024,512]{1,0:T(8,128)} %get-tuple-element.46.weighted), custom_call_target="tpu_custom_call" | custom-call | flops 6600000000 | bytes 4096 | tf_op jit(solution)/shard_map/update0/pallas_call | solution.py:294
  65.4 4.2 %collective-permute-start.11 = (f32[192,512]{1,0:T(8,128)S(1)}, f32[192,512]{1,0:T(8,128)S(1)}, u32[]{:S(2)}, u32[]{:S(2)}) collective-permute-start(f32[192,512]{1,0:T(8,128)S(1)} %constant_dynamic-update-slice_fusion.refs_0_), channel_id=1, source_target_pairs={{0,4},{1,5},{2,6},{3,7},{4,0},{5,1},{6,2},{7,3},{8,12},{9,13},{10,... | collective-permute-start | bytes 1179656 | tf_op jit(solution)/shard_map/ppermute | solution.py:308
  73.3 5.9 %collective-permute-done.34.same = f32[640,128]{1,0:T(8,128)S(1)} collective-permute-done((f32[640,128]{1,0:T(8,128)S(1)}, f32[640,128]{1,0:T(8,128)S(1)}, u32[]{:S(2)}, u32[]{:S(2)}) %collective-permute-start.34) | collective-permute-done | bytes 327712 | tf_op jit(solution)/shard_map/ppermute | solution.py:308
  79.3 4.2 %collective-permute-start.40 = (f32[576,128]{1,0:T(8,128)}, f32[576,128]{1,0:T(8,128)}, u32[]{:S(2)}, u32[]{:S(2)}) collective-permute-start(f32[576,128]{1,0:T(8,128)} %collective-permute-done.36.refs_0_), channel_id=1, source_target_pairs={{0,4},{1,5},{2,6},{3,7},{4,0},{5,1},{6,2},{7,3},{8,12},{9,13},{10,... | collective-permute-start | bytes 884744 | tf_op jit(solution)/shard_map/ppermute | solution.py:308
  83.5 4.7 %collective-permute-done.11.refs_4_ = f32[192,512]{1,0:T(8,128)S(1)} collective-permute-done((f32[192,512]{1,0:T(8,128)S(1)}, f32[192,512]{1,0:T(8,128)S(1)}, u32[]{:S(2)}, u32[]{:S(2)}) %collective-permute-start.11) | collective-permute-done | bytes 393248 | tf_op jit(solution)/shard_map/ppermute | solution.py:308
  95.1 4.2 %collective-permute-done.40.refs_4_ = f32[576,128]{1,0:T(8,128)} collective-permute-done((f32[576,128]{1,0:T(8,128)}, f32[576,128]{1,0:T(8,128)}, u32[]{:S(2)}, u32[]{:S(2)}) %collective-permute-start.40) | collective-permute-done | bytes 294944 | tf_op jit(solution)/shard_map/ppermute | solution.py:308
  100.0 5.2 %collective-permute-done.42.refs_6_ = f32[576,128]{1,0:T(8,128)} collective-permute-done((f32[576,128]{1,0:T(8,128)}, f32[576,128]{1,0:T(8,128)}, u32[]{:S(2)}, u32[]{:S(2)}) %collective-permute-start.42) | collective-permute-done | bytes 294944 | tf_op jit(solution)/shard_map/ppermute | solution.py:308
  106.6 3.8 %place1.1 = (f32[512,512]{1,0:T(8,128)}, f32[1024,512]{1,0:T(8,128)}) custom-call(s32[3]{0:T(128)} %get-tuple-element.79.place, f32[192,512]{1,0:T(8,128)} %copy-done.3, f32[192,512]{1,0:T(8,128)} %copy-done.13, f32[192,512]{1,0:T(8,128)} %copy-done.10, f32[192,512]{1,0:T(8,128)} %copy-done.14, f32[192,512]{1,0:T(8,128)} %copy-done.11, ...), custom_call_target="tpu_custom_call" | custom-call | flops 3300000000 | bytes 4096 | tf_op jit(solution)/shard_map/place1/pallas_call | solution.py:294
  112.1 17.4 %factor1.1.inverse = f32[512,512]{1,0:T(8,128)} custom-call(s32[3]{0:T(128)} %get-tuple-element.79.place, f32[512,512]{1,0:T(8,128)} %get-tuple-element.40.pivot, f32[1280,128]{1,0:T(8,128)} %get-tuple-element.43.mine, f32[640,128]{1,0:T(8,128)} %copy-done.34, f32[640,128]{1,0:T(8,128)} %copy-done.39), custom_call_target="tpu_custom_call" | custom-call | flops 19800000512 | bytes 4096 | tf_op jit(solution)/shard_map/factor1/pallas_call | solution.py:294
  130.6 10.9 %columns1.1 = (f32[1024,512]{1,0:T(8,128)}, f32[1024,512]{1,0:T(8,128)}, f32[1280,128]{1,0:T(8,128)}, f32[640,128]{1,0:T(8,128)}, f32[8192,128]{1,0:T(8,128)}) custom-call(s32[3]{0:T(128)} %get-tuple-element.79.place, s32[72]{0:T(128)} %concatenate.24.tables, f32[512,512]{1,0:T(8,128)} %factor1.1.inverse, f32[1024,512]{1,0:T(8,128)} %get-tuple-element.45.below, ...), custom_call_target="tpu_custom_call" | custom-call | flops 11000000512 | bytes 4096 | tf_op jit(solution)/shard_map/columns1/pallas_call | solution.py:294
  141.5 15.0 %update1.1 = (f32[8192,128]{1,0:T(8,128)}, f32[576,128]{1,0:T(8,128)}) custom-call(s32[3]{0:T(128)} %get-tuple-element.79.place, s32[72]{0:T(128)} %concatenate.24.tables, f32[1024,512]{1,0:T(8,128)} %get-tuple-element.52.columns, f32[1024,512]{1,0:T(8,128)} %get-tuple-element.53.weighted, f32[8192,128]{1,0:T(8,128)} %get-tuple-element.47.mine, ...), custom_call_target="tpu_custom_call" | custom-call | flops 8800000000 | bytes 4096 | tf_op jit(solution)/shard_map/update1/pallas_call | solution.py:294
  163.7 15.0 %collective-permute-done.16 = f32[96,512]{1,0:T(8,128)S(1)} collective-permute-done((f32[96,512]{1,0:T(8,128)S(1)}, f32[96,512]{1,0:T(8,128)S(1)}, u32[]{:S(2)}, u32[]{:S(2)}) %collective-permute-start.16) | collective-permute-done | bytes 196640 | tf_op jit(solution)/shard_map/ppermute | solution.py:308
  185.6 20.1 %collective-permute-done.48.refs_2_ = f32[576,128]{1,0:T(8,128)S(1)} collective-permute-done((f32[576,128]{1,0:T(8,128)S(1)}, f32[576,128]{1,0:T(8,128)S(1)}, u32[]{:S(2)}, u32[]{:S(2)}) %collective-permute-start.48) | collective-permute-done | bytes 294944 | tf_op jit(solution)/shard_map/ppermute | solution.py:308
  206.7 3.8 %collective-permute-done.50.refs_4_ = f32[576,128]{1,0:T(8,128)S(1)} collective-permute-done((f32[576,128]{1,0:T(8,128)S(1)}, f32[576,128]{1,0:T(8,128)S(1)}, u32[]{:S(2)}, u32[]{:S(2)}) %collective-permute-start.50) | collective-permute-done | bytes 294944 | tf_op jit(solution)/shard_map/ppermute | solution.py:308
  213.2 6.1 %collective-permute-done.52.refs_6_ = f32[576,128]{1,0:T(8,128)S(1)} collective-permute-done((f32[576,128]{1,0:T(8,128)S(1)}, f32[576,128]{1,0:T(8,128)S(1)}, u32[]{:S(2)}, u32[]{:S(2)}) %collective-permute-start.52) | collective-permute-done | bytes 294944 | tf_op jit(solution)/shard_map/ppermute | solution.py:308
  221.3 3.8 %place2.1 = (f32[512,512]{1,0:T(8,128)}, f32[1024,512]{1,0:T(8,128)}) custom-call(s32[3]{0:T(128)} %get-tuple-element.80.place, f32[192,512]{1,0:T(8,128)} %copy-done.4, f32[192,512]{1,0:T(8,128)} %copy-done.27, f32[192,512]{1,0:T(8,128)} %copy-done.20, f32[192,512]{1,0:T(8,128)} %copy-done.29, f32[192,512]{1,0:T(8,128)} %copy-done.23, ...), custom_call_target="tpu_custom_call" | custom-call | flops 3300000000 | bytes 4096 | tf_op jit(solution)/shard_map/place2/pallas_call | solution.py:294
  225.8 17.3 %factor2.1.inverse = f32[512,512]{1,0:T(8,128)} custom-call(s32[3]{0:T(128)} %get-tuple-element.80.place, f32[512,512]{1,0:T(8,128)} %get-tuple-element.39.pivot, f32[1280,128]{1,0:T(8,128)} %get-tuple-element.49.mine, f32[640,128]{1,0:T(8,128)} %copy-done.36, f32[640,128]{1,0:T(8,128)} %copy-done.40), custom_call_target="tpu_custom_call" | custom-call | flops 19800000512 | bytes 4096 | tf_op jit(solution)/shard_map/factor2/pallas_call | solution.py:294
  244.2 11.0 %columns2.1 = (f32[1024,512]{1,0:T(8,128)}, f32[1024,512]{1,0:T(8,128)}, f32[1280,128]{1,0:T(8,128)}, f32[640,128]{1,0:T(8,128)}, f32[8192,128]{1,0:T(8,128)}) custom-call(s32[3]{0:T(128)} %get-tuple-element.80.place, s32[72]{0:T(128)} %concatenate.24.tables, f32[512,512]{1,0:T(8,128)} %factor2.1.inverse, f32[1024,512]{1,0:T(8,128)} %get-tuple-element.51.below, ...), custom_call_target="tpu_custom_call" | custom-call | flops 11000000512 | bytes 4096 | tf_op jit(solution)/shard_map/columns2/pallas_call | solution.py:294
  255.2 15.0 %update2.1 = (f32[8192,128]{1,0:T(8,128)}, f32[576,128]{1,0:T(8,128)}) custom-call(s32[3]{0:T(128)} %get-tuple-element.80.place, s32[72]{0:T(128)} %concatenate.24.tables, f32[1024,512]{1,0:T(8,128)} %get-tuple-element.60.columns, f32[1024,512]{1,0:T(8,128)} %get-tuple-element.61.weighted, f32[8192,128]{1,0:T(8,128)} %get-tuple-element.55.mine, ...), custom_call_target="tpu_custom_call" | custom-call | flops 8800000000 | bytes 4096 | tf_op jit(solution)/shard_map/update2/pallas_call | solution.py:294
  280.1 10.6 %collective-permute-done.26 = f32[96,512]{1,0:T(8,128)S(1)} collective-permute-done((f32[96,512]{1,0:T(8,128)S(1)}, f32[96,512]{1,0:T(8,128)S(1)}, u32[]{:S(2)}, u32[]{:S(2)}) %collective-permute-start.26) | collective-permute-done | bytes 196640 | tf_op jit(solution)/shard_map/ppermute | solution.py:308
  290.8 4.1 %collective-permute-start.30 = (f32[192,512]{1,0:T(8,128)S(1)}, f32[192,512]{1,0:T(8,128)S(1)}, u32[]{:S(2)}, u32[]{:S(2)}) collective-permute-start(f32[192,512]{1,0:T(8,128)S(1)} %constant_dynamic-update-slice_fusion.5.refs_0_), channel_id=1, source_target_pairs={{0,4},{1,5},{2,6},{3,7},{4,0},{5,1},{6,2},{7,3},{8,12},{9,13},{10,... | collective-permute-start | bytes 1179656 | tf_op jit(solution)/shard_map/ppermute | solution.py:308
  295.5 4.1 %collective-permute-start.60 = (f32[576,128]{1,0:T(8,128)S(1)}, f32[576,128]{1,0:T(8,128)S(1)}, u32[]{:S(2)}, u32[]{:S(2)}) collective-permute-start(f32[576,128]{1,0:T(8,128)S(1)} %collective-permute-done.56.refs_0_), channel_id=1, source_target_pairs={{0,4},{1,5},{2,6},{3,7},{4,0},{5,1},{6,2},{7,3},{8,12},{9,13},{10,... | collective-permute-start | bytes 884744 | tf_op jit(solution)/shard_map/ppermute | solution.py:308
  299.6 18.0 %collective-permute-done.58.refs_2_ = f32[576,128]{1,0:T(8,128)S(1)} collective-permute-done((f32[576,128]{1,0:T(8,128)S(1)}, f32[576,128]{1,0:T(8,128)S(1)}, u32[]{:S(2)}, u32[]{:S(2)}) %collective-permute-start.58) | collective-permute-done | bytes 294944 | tf_op jit(solution)/shard_map/ppermute | solution.py:308
  318.6 5.7 %collective-permute-done.60.refs_4_ = f32[576,128]{1,0:T(8,128)S(1)} collective-permute-done((f32[576,128]{1,0:T(8,128)S(1)}, f32[576,128]{1,0:T(8,128)S(1)}, u32[]{:S(2)}, u32[]{:S(2)}) %collective-permute-start.60) | collective-permute-done | bytes 294944 | tf_op jit(solution)/shard_map/ppermute | solution.py:308
  324.9 8.0 %collective-permute-done.62.refs_6_ = f32[576,128]{1,0:T(8,128)S(1)} collective-permute-done((f32[576,128]{1,0:T(8,128)S(1)}, f32[576,128]{1,0:T(8,128)S(1)}, u32[]{:S(2)}, u32[]{:S(2)}) %collective-permute-start.62) | collective-permute-done | bytes 294944 | tf_op jit(solution)/shard_map/ppermute | solution.py:308
  334.6 3.8 %place3.1 = (f32[512,512]{1,0:T(8,128)}, f32[1024,512]{1,0:T(8,128)}) custom-call(s32[3]{0:T(128)} %get-tuple-element.81.place, f32[192,512]{1,0:T(8,128)} %copy-done.5, f32[192,512]{1,0:T(8,128)} %copy-done.26, f32[192,512]{1,0:T(8,128)} %copy-done.19, f32[192,512]{1,0:T(8,128)} %copy-done.28, f32[192,512]{1,0:T(8,128)} %copy-done.21, ...), custom_call_target="tpu_custom_call" | custom-call | flops 3300000000 | bytes 4096 | tf_op jit(solution)/shard_map/place3/pallas_call | solution.py:294
  339.2 17.4 %factor3.1.inverse = f32[512,512]{1,0:T(8,128)} custom-call(s32[3]{0:T(128)} %get-tuple-element.81.place, f32[512,512]{1,0:T(8,128)} %get-tuple-element.38.pivot, f32[1280,128]{1,0:T(8,128)} %get-tuple-element.57.mine, f32[640,128]{1,0:T(8,128)} %copy-done.35, f32[640,128]{1,0:T(8,128)} %copy-done.41), custom_call_target="tpu_custom_call" | custom-call | flops 19800000512 | bytes 4096 | tf_op jit(solution)/shard_map/factor3/pallas_call | solution.py:294
  357.6 6.5 %last.1 = f32[16,1024]{1,0:T(8,128)} custom-call(s32[3]{0:T(128)} %get-tuple-element.81.place, s32[72]{0:T(128)} %concatenate.24.tables, f32[512,512]{1,0:T(8,128)} %factor3.1.inverse, f32[1024,512]{1,0:T(8,128)} %get-tuple-element.59.below, f32[8192,128]{1,0:T(8,128)} %get-tuple-element.63.mine, f32[576,128]{1,0:T(8,128)} %copy-done.43, ...), custom_call_target="tpu_custom_call" | custom-call | flops 8800000000 | bytes 4096 | tf_op jit(solution)/shard_map/last/pallas_call | solution.py:294
  (259 shorter events, 68.6 us)
Async XLA Ops:
  1.9 20.1 %collective-permute-start.5 = (f32[192,512]{1,0:T(8,128)}, f32[192,512]{1,0:T(8,128)S(1)}, u32[]{:S(2)}, u32[]{:S(2)}) collective-permute-start(f32[192,512]{1,0:T(8,128)} %refs_0_.1), channel_id=1, source_target_pairs={{0,6},{1,7},{2,4},{3,5},{4,2},{5,3},{6,0},{7,1},{8,14},{9,15},{10,... | collective-permute-start | bytes 1179656 | tf_op jit(solution)/shard_map/ppermute | solution.py:308
  23.6 41.6 %collective-permute-start.7 = (f32[96,512]{1,0:T(8,128)}, f32[96,512]{1,0:T(8,128)S(1)}, u32[]{:S(2)}, u32[]{:S(2)}) collective-permute-start(f32[96,512]{1,0:T(8,128)} %param.8), channel_id=1, source_target_pairs={{0,8},{8,0},{16,24},{24,16},{32,40},{40,32},{48,56},{56,48},{64,72... | collective-permute-start | bytes 589832 | tf_op jit(solution)/shard_map/ppermute | solution.py:308
  65.4 22.7 %collective-permute-start.11 = (f32[192,512]{1,0:T(8,128)S(1)}, f32[192,512]{1,0:T(8,128)S(1)}, u32[]{:S(2)}, u32[]{:S(2)}) collective-permute-start(f32[192,512]{1,0:T(8,128)S(1)} %constant_dynamic-update-slice_fusion.refs_0_), channel_id=1, source_target_pairs={{0,4},{1,5},{2,6},{3,7},{4,0},{5,1},{6,2},{7,3},{8,12},{9,13},{10,... | collective-permute-start | bytes 1179656 | tf_op jit(solution)/shard_map/ppermute | solution.py:308
  79.3 20.1 %collective-permute-start.40 = (f32[576,128]{1,0:T(8,128)}, f32[576,128]{1,0:T(8,128)}, u32[]{:S(2)}, u32[]{:S(2)}) collective-permute-start(f32[576,128]{1,0:T(8,128)} %collective-permute-done.36.refs_0_), channel_id=1, source_target_pairs={{0,4},{1,5},{2,6},{3,7},{4,0},{5,1},{6,2},{7,3},{8,12},{9,13},{10,... | collective-permute-start | bytes 884744 | tf_op jit(solution)/shard_map/ppermute | solution.py:308
  105.2 24.4 %collective-permute-start.37 = (f32[576,128]{1,0:T(8,128)}, f32[576,128]{1,0:T(8,128)S(1)}, u32[]{:S(2)}, u32[]{:S(2)}) collective-permute-start(f32[576,128]{1,0:T(8,128)} %collective-permute-done.36.refs_0_), channel_id=1, source_target_pairs={{0,1},{1,0},{2,3},{3,2},{4,5},{5,4},{6,7},{7,6},{8,9},{9,8},{10,11... | collective-permute-start | bytes 884744 | tf_op jit(solution)/shard_map/ppermute | solution.py:308
  105.2 24.4 %collective-permute-start.39 = (f32[576,128]{1,0:T(8,128)}, f32[576,128]{1,0:T(8,128)S(1)}, u32[]{:S(2)}, u32[]{:S(2)}) collective-permute-start(f32[576,128]{1,0:T(8,128)} %collective-permute-done.38.refs_2_), channel_id=1, source_target_pairs={{0,1},{1,0},{2,3},{3,2},{4,5},{5,4},{6,7},{7,6},{8,9},{9,8},{10,11... | collective-permute-start | bytes 884744 | tf_op jit(solution)/shard_map/ppermute | solution.py:308
  105.7 23.9 %collective-permute-start.41 = (f32[576,128]{1,0:T(8,128)}, f32[576,128]{1,0:T(8,128)S(1)}, u32[]{:S(2)}, u32[]{:S(2)}) collective-permute-start(f32[576,128]{1,0:T(8,128)} %collective-permute-done.40.refs_4_), channel_id=1, source_target_pairs={{0,1},{1,0},{2,3},{3,2},{4,5},{5,4},{6,7},{7,6},{8,9},{9,8},{10,11... | collective-permute-start | bytes 884744 | tf_op jit(solution)/shard_map/ppermute | solution.py:308
  105.8 23.8 %collective-permute-start.43 = (f32[576,128]{1,0:T(8,128)}, f32[576,128]{1,0:T(8,128)S(1)}, u32[]{:S(2)}, u32[]{:S(2)}) collective-permute-start(f32[576,128]{1,0:T(8,128)} %collective-permute-done.42.refs_6_), channel_id=1, source_target_pairs={{0,1},{1,0},{2,3},{3,2},{4,5},{5,4},{6,7},{7,6},{8,9},{9,8},{10,11... | collective-permute-start | bytes 884744 | tf_op jit(solution)/shard_map/ppermute | solution.py:308
  110.5 49.7 %collective-permute-start.15 = (f32[48,512]{1,0:T(8,128)S(1)}, f32[48,512]{1,0:T(8,128)S(1)}, u32[]{:S(2)}, u32[]{:S(2)}) collective-permute-start(f32[48,512]{1,0:T(8,128)S(1)} %copy-done.1), channel_id=1, source_target_pairs={{0,8},{8,0},{16,24},{24,16},{32,40},{40,32},{48,56},{56,48},{64,72... | collective-permute-start | bytes 294920 | tf_op jit(solution)/shard_map/ppermute | solution.py:308
  156.5 27.1 %collective-permute-start.46 = (f32[576,128]{1,0:T(8,128)}, f32[576,128]{1,0:T(8,128)S(1)}, u32[]{:S(2)}, u32[]{:S(2)}) collective-permute-start(f32[576,128]{1,0:T(8,128)} %get-tuple-element.56), channel_id=1, source_target_pairs={{0,16},{8,24},{16,0},{24,8},{32,48},{40,56},{48,32},{56,40},{64,80... | collective-permute-start | bytes 884744 | tf_op jit(solution)/shard_map/ppermute | solution.py:308
  160.1 23.5 %collective-permute-start.44 = (f32[640,128]{1,0:T(8,128)S(1)}, f32[640,128]{1,0:T(8,128)S(1)}, u32[]{:S(2)}, u32[]{:S(2)}) collective-permute-start(f32[640,128]{1,0:T(8,128)S(1)} %copy-done.38), channel_id=1, source_target_pairs={{0,16},{8,24},{16,0},{24,8},{32,48},{40,56},{48,32},{56,40},{64,80... | collective-permute-start | bytes 983048 | tf_op jit(solution)/shard_map/ppermute | solution.py:308
  178.8 26.9 %collective-permute-start.18 = (f32[192,512]{1,0:T(8,128)S(1)}, f32[192,512]{1,0:T(8,128)S(1)}, u32[]{:S(2)}, u32[]{:S(2)}) collective-permute-start(f32[192,512]{1,0:T(8,128)S(1)} %constant_dynamic-update-slice_fusion.2.refs_0_), channel_id=1, source_target_pairs={{0,2},{1,3},{2,0},{3,1},{4,6},{5,7},{6,4},{7,5},{8,10},{9,11},{10,... | collective-permute-start | bytes 1179656 | tf_op jit(solution)/shard_map/ppermute | solution.py:308
  178.9 27.3 %collective-permute-start.20 = (f32[192,512]{1,0:T(8,128)S(1)}, f32[192,512]{1,0:T(8,128)S(1)}, u32[]{:S(2)}, u32[]{:S(2)}) collective-permute-start(f32[192,512]{1,0:T(8,128)S(1)} %constant_dynamic-update-slice_fusion.2.refs_0_), channel_id=1, source_target_pairs={{0,4},{1,5},{2,6},{3,7},{4,0},{5,1},{6,2},{7,3},{8,12},{9,13},{10,... | collective-permute-start | bytes 1179656 | tf_op jit(solution)/shard_map/ppermute | solution.py:308
  180.9 25.4 %collective-permute-start.22 = (f32[192,512]{1,0:T(8,128)S(1)}, f32[192,512]{1,0:T(8,128)S(1)}, u32[]{:S(2)}, u32[]{:S(2)}) collective-permute-start(f32[192,512]{1,0:T(8,128)S(1)} %constant_dynamic-update-slice_fusion.2.refs_0_), channel_id=1, source_target_pairs={{0,6},{1,7},{2,4},{3,5},{4,2},{5,3},{6,0},{7,1},{8,14},{9,15},{10,... | collective-permute-start | bytes 1179656 | tf_op jit(solution)/shard_map/ppermute | solution.py:308
  183.6 22.1 %collective-permute-start.48 = (f32[576,128]{1,0:T(8,128)S(1)}, f32[576,128]{1,0:T(8,128)S(1)}, u32[]{:S(2)}, u32[]{:S(2)}) collective-permute-start(f32[576,128]{1,0:T(8,128)S(1)} %collective-permute-done.46.refs_0_), channel_id=1, source_target_pairs={{0,2},{1,3},{2,0},{3,1},{4,6},{5,7},{6,4},{7,5},{8,10},{9,11},{10,... | collective-permute-start | bytes 884744 | tf_op jit(solution)/shard_map/ppermute | solution.py:308
  183.6 26.9 %collective-permute-start.50 = (f32[576,128]{1,0:T(8,128)S(1)}, f32[576,128]{1,0:T(8,128)S(1)}, u32[]{:S(2)}, u32[]{:S(2)}) collective-permute-start(f32[576,128]{1,0:T(8,128)S(1)} %collective-permute-done.46.refs_0_), channel_id=1, source_target_pairs={{0,4},{1,5},{2,6},{3,7},{4,0},{5,1},{6,2},{7,3},{8,12},{9,13},{10,... | collective-permute-start | bytes 884744 | tf_op jit(solution)/shard_map/ppermute | solution.py:308
  219.3 23.8 %collective-permute-start.47 = (f32[576,128]{1,0:T(8,128)S(1)}, f32[576,128]{1,0:T(8,128)S(1)}, u32[]{:S(2)}, u32[]{:S(2)}) collective-permute-start(f32[576,128]{1,0:T(8,128)S(1)} %collective-permute-done.46.refs_0_), channel_id=1, source_target_pairs={{0,1},{1,0},{2,3},{3,2},{4,5},{5,4},{6,7},{7,6},{8,9},{9,8},{10,11... | collective-permute-start | bytes 884744 | tf_op jit(solution)/shard_map/ppermute | solution.py:308
  220.0 23.2 %collective-permute-start.49 = (f32[576,128]{1,0:T(8,128)S(1)}, f32[576,128]{1,0:T(8,128)S(1)}, u32[]{:S(2)}, u32[]{:S(2)}) collective-permute-start(f32[576,128]{1,0:T(8,128)S(1)} %collective-permute-done.48.refs_2_), channel_id=1, source_target_pairs={{0,1},{1,0},{2,3},{3,2},{4,5},{5,4},{6,7},{7,6},{8,9},{9,8},{10,11... | collective-permute-start | bytes 884744 | tf_op jit(solution)/shard_map/ppermute | solution.py:308
  220.1 23.1 %collective-permute-start.51 = (f32[576,128]{1,0:T(8,128)S(1)}, f32[576,128]{1,0:T(8,128)S(1)}, u32[]{:S(2)}, u32[]{:S(2)}) collective-permute-start(f32[576,128]{1,0:T(8,128)S(1)} %collective-permute-done.50.refs_4_), channel_id=1, source_target_pairs={{0,1},{1,0},{2,3},{3,2},{4,5},{5,4},{6,7},{7,6},{8,9},{9,8},{10,11... | collective-permute-start | bytes 884744 | tf_op jit(solution)/shard_map/ppermute | solution.py:308
  220.5 22.7 %collective-permute-start.53 = (f32[576,128]{1,0:T(8,128)S(1)}, f32[576,128]{1,0:T(8,128)S(1)}, u32[]{:S(2)}, u32[]{:S(2)}) collective-permute-start(f32[576,128]{1,0:T(8,128)S(1)} %collective-permute-done.52.refs_6_), channel_id=1, source_target_pairs={{0,1},{1,0},{2,3},{3,2},{4,5},{5,4},{6,7},{7,6},{8,9},{9,8},{10,11... | collective-permute-start | bytes 884744 | tf_op jit(solution)/shard_map/ppermute | solution.py:308
  225.1 47.1 %collective-permute-start.24 = (f32[24,512]{1,0:T(8,128)S(1)}, f32[24,512]{1,0:T(8,128)S(1)}, u32[]{:S(2)}, u32[]{:S(2)}) collective-permute-start(f32[24,512]{1,0:T(8,128)S(1)} %copy-done), channel_id=1, source_target_pairs={{0,8},{8,0},{16,24},{24,16},{32,40},{40,32},{48,56},{56,48},{64,72... | collective-permute-start | bytes 147464 | tf_op jit(solution)/shard_map/ppermute | solution.py:308
  270.1 25.3 %collective-permute-start.56 = (f32[576,128]{1,0:T(8,128)}, f32[576,128]{1,0:T(8,128)S(1)}, u32[]{:S(2)}, u32[]{:S(2)}) collective-permute-start(f32[576,128]{1,0:T(8,128)} %get-tuple-element.64), channel_id=1, source_target_pairs={{0,32},{8,40},{16,48},{24,56},{32,0},{40,8},{48,16},{56,24},{64,96... | collective-permute-start | bytes 884744 | tf_op jit(solution)/shard_map/ppermute | solution.py:308
  271.7 23.7 %collective-permute-start.54 = (f32[640,128]{1,0:T(8,128)S(1)}, f32[640,128]{1,0:T(8,128)S(1)}, u32[]{:S(2)}, u32[]{:S(2)}) collective-permute-start(f32[640,128]{1,0:T(8,128)S(1)} %copy-done.37), channel_id=1, source_target_pairs={{0,32},{8,40},{16,48},{24,56},{32,0},{40,8},{48,16},{56,24},{64,96... | collective-permute-start | bytes 983048 | tf_op jit(solution)/shard_map/ppermute | solution.py:308
  290.7 26.9 %collective-permute-start.28 = (f32[192,512]{1,0:T(8,128)S(1)}, f32[192,512]{1,0:T(8,128)S(1)}, u32[]{:S(2)}, u32[]{:S(2)}) collective-permute-start(f32[192,512]{1,0:T(8,128)S(1)} %constant_dynamic-update-slice_fusion.5.refs_0_), channel_id=1, source_target_pairs={{0,2},{1,3},{2,0},{3,1},{4,6},{5,7},{6,4},{7,5},{8,10},{9,11},{10,... | collective-permute-start | bytes 1179656 | tf_op jit(solution)/shard_map/ppermute | solution.py:308
  290.8 27.3 %collective-permute-start.30 = (f32[192,512]{1,0:T(8,128)S(1)}, f32[192,512]{1,0:T(8,128)S(1)}, u32[]{:S(2)}, u32[]{:S(2)}) collective-permute-start(f32[192,512]{1,0:T(8,128)S(1)} %constant_dynamic-update-slice_fusion.5.refs_0_), channel_id=1, source_target_pairs={{0,4},{1,5},{2,6},{3,7},{4,0},{5,1},{6,2},{7,3},{8,12},{9,13},{10,... | collective-permute-start | bytes 1179656 | tf_op jit(solution)/shard_map/ppermute | solution.py:308
  294.9 23.3 %collective-permute-start.32 = (f32[192,512]{1,0:T(8,128)S(1)}, f32[192,512]{1,0:T(8,128)S(1)}, u32[]{:S(2)}, u32[]{:S(2)}) collective-permute-start(f32[192,512]{1,0:T(8,128)S(1)} %constant_dynamic-update-slice_fusion.5.refs_0_), channel_id=1, source_target_pairs={{0,6},{1,7},{2,4},{3,5},{4,2},{5,3},{6,0},{7,1},{8,14},{9,15},{10,... | collective-permute-start | bytes 1179656 | tf_op jit(solution)/shard_map/ppermute | solution.py:308
  295.5 22.1 %collective-permute-start.58 = (f32[576,128]{1,0:T(8,128)S(1)}, f32[576,128]{1,0:T(8,128)S(1)}, u32[]{:S(2)}, u32[]{:S(2)}) collective-permute-start(f32[576,128]{1,0:T(8,128)S(1)} %collective-permute-done.56.refs_0_), channel_id=1, source_target_pairs={{0,2},{1,3},{2,0},{3,1},{4,6},{5,7},{6,4},{7,5},{8,10},{9,11},{10,... | collective-permute-start | bytes 884744 | tf_op jit(solution)/shard_map/ppermute | solution.py:308
  295.5 28.8 %collective-permute-start.60 = (f32[576,128]{1,0:T(8,128)S(1)}, f32[576,128]{1,0:T(8,128)S(1)}, u32[]{:S(2)}, u32[]{:S(2)}) collective-permute-start(f32[576,128]{1,0:T(8,128)S(1)} %collective-permute-done.56.refs_0_), channel_id=1, source_target_pairs={{0,4},{1,5},{2,6},{3,7},{4,0},{5,1},{6,2},{7,3},{8,12},{9,13},{10,... | collective-permute-start | bytes 884744 | tf_op jit(solution)/shard_map/ppermute | solution.py:308
  332.8 23.8 %collective-permute-start.57 = (f32[576,128]{1,0:T(8,128)S(1)}, f32[576,128]{1,0:T(8,128)S(1)}, u32[]{:S(2)}, u32[]{:S(2)}) collective-permute-start(f32[576,128]{1,0:T(8,128)S(1)} %collective-permute-done.56.refs_0_), channel_id=1, source_target_pairs={{0,1},{1,0},{2,3},{3,2},{4,5},{5,4},{6,7},{7,6},{8,9},{9,8},{10,11... | collective-permute-start | bytes 884744 | tf_op jit(solution)/shard_map/ppermute | solution.py:308
  333.4 23.3 %collective-permute-start.59 = (f32[576,128]{1,0:T(8,128)S(1)}, f32[576,128]{1,0:T(8,128)S(1)}, u32[]{:S(2)}, u32[]{:S(2)}) collective-permute-start(f32[576,128]{1,0:T(8,128)S(1)} %collective-permute-done.58.refs_2_), channel_id=1, source_target_pairs={{0,1},{1,0},{2,3},{3,2},{4,5},{5,4},{6,7},{7,6},{8,9},{9,8},{10,11... | collective-permute-start | bytes 884744 | tf_op jit(solution)/shard_map/ppermute | solution.py:308
  333.5 23.2 %collective-permute-start.61 = (f32[576,128]{1,0:T(8,128)S(1)}, f32[576,128]{1,0:T(8,128)S(1)}, u32[]{:S(2)}, u32[]{:S(2)}) collective-permute-start(f32[576,128]{1,0:T(8,128)S(1)} %collective-permute-done.60.refs_4_), channel_id=1, source_target_pairs={{0,1},{1,0},{2,3},{3,2},{4,5},{5,4},{6,7},{7,6},{8,9},{9,8},{10,11... | collective-permute-start | bytes 884744 | tf_op jit(solution)/shard_map/ppermute | solution.py:308
  333.9 22.8 %collective-permute-start.63 = (f32[576,128]{1,0:T(8,128)S(1)}, f32[576,128]{1,0:T(8,128)S(1)}, u32[]{:S(2)}, u32[]{:S(2)}) collective-permute-start(f32[576,128]{1,0:T(8,128)S(1)} %collective-permute-done.62.refs_6_), channel_id=1, source_target_pairs={{0,1},{1,0},{2,3},{3,2},{4,5},{5,4},{6,7},{7,6},{8,9},{9,8},{10,11... | collective-permute-start | bytes 884744 | tf_op jit(solution)/shard_map/ppermute | solution.py:308
  (95 other events, 1263.1 us)
